TPU v7x, 768 devices: a whole 4x8x12 slice. The times are simulated.
768 devices in a mesh: dp: 24 (over x, z_lo, core), fsdp: 32 (over y, z_hi).
Axes of the slice: x: 4, y: 8, z: 12 (z_hi: 4, z_lo: 3; z = z_hi * 3 + z_lo), core: 2. Of those that a mesh axis runs over, the one named last changes fastest.
Arguments:
- student_feat: bfloat16 [18432, 384], P('dp', 'fsdp'), may hold values from -0.3984375 to 0.3984375
- teacher_feat: bfloat16 [4608, 384], P('dp', 'fsdp'), may hold values from -0.3984375 to 0.3984375
- student_proto: bfloat16 [384, 65536], P(None, 'fsdp'), may hold values from -5 to 5
- teacher_proto: float32 [384, 65536], P('dp', 'fsdp'), may hold values from -5 to 5
- center: float32 [65536], P('fsdp'), may hold values from -0.1 to 0.1
Outputs:
- new_teacher: float32 [384, 65536], P('dp', 'fsdp')
- grad_student_feat: float32 [18432, 384], P('dp')
- grad_student_proto: float32 [384, 65536], P('dp', 'fsdp')
All inputs are finite; a program needn't handle non-finite values.
Results may differ from a plain program's by a relative error of at most 0.005.
The roundings to bfloat16 on the way count: a program that leaves them out, or rounds other values in their place, can miss the bound.
Values may be sent and summed in bfloat16 or wider, within the bound.
A program may use at most 32 MiB of HBM per device.

v0:
```python
import jax
import jax.numpy as jnp
from jax import lax
from jax.sharding import PartitionSpec as P

PROTO = 65536
STUDENT_CROPS = 8
GLOBAL_CROPS = 2


epsilon = 1e-06
momentum = 0.994
teacher_temp = 0.04
student_temp = 0.1


def unit_rows(values):
    inverse = lax.rsqrt(jnp.sum(values * values, axis=1, keepdims=True) + epsilon)
    return (values * inverse, inverse)


def unit_columns(values):
    inverse = lax.rsqrt(jnp.sum(values * values, axis=0, keepdims=True) + epsilon)
    return (values * inverse, inverse)


def crop_grads(teacher_prob, student_prob):
    images = teacher_prob.shape[0] // GLOBAL_CROPS
    proto_count = teacher_prob.shape[1]
    teacher_view = teacher_prob.reshape(images, GLOBAL_CROPS, proto_count)
    student_view = student_prob.reshape(images, STUDENT_CROPS, proto_count)
    pair_sum = jnp.sum(teacher_view, axis=1, keepdims=True)
    partner = jnp.concatenate(
        [
            pair_sum - teacher_view,
            jnp.broadcast_to(pair_sum, (images, STUDENT_CROPS - GLOBAL_CROPS, proto_count)),
        ],
        axis=1,
    )
    position = lax.broadcasted_iota(jnp.int32, (1, STUDENT_CROPS, 1), 1)
    counts = jnp.where(
        position < GLOBAL_CROPS, jnp.float32(GLOBAL_CROPS - 1), jnp.float32(GLOBAL_CROPS)
    )
    loss_scale = jnp.float32(PROTO / 16.0)
    logit_grads = loss_scale * (counts * student_view - partner) / student_temp
    return logit_grads.reshape(images * STUDENT_CROPS, proto_count).astype(jnp.bfloat16)


def body(student_feat, teacher_feat, student_proto, teacher_proto, center):
    student_full, teacher_full = (
        lax.all_gather(student_feat, "fsdp", axis=1, tiled=True),
        lax.all_gather(teacher_feat, "fsdp", axis=1, tiled=True),
    )
    student_unit, student_inv = unit_rows(student_full.astype(jnp.float32))
    student_rows = student_unit.astype(jnp.bfloat16)
    teacher_unit, teacher_inv = unit_rows(teacher_full.astype(jnp.float32))
    teacher_rows = teacher_unit.astype(jnp.bfloat16)
    proto_unit, proto_inv = unit_columns(student_proto.astype(jnp.float32))
    proto_half = proto_unit.astype(jnp.bfloat16)
    own_count = teacher_proto.shape[0]
    own_start = lax.axis_index("dp") * own_count
    student_own = lax.dynamic_slice_in_dim(student_proto, own_start, own_count, 0).astype(
        jnp.float32
    )
    new_teacher = momentum * teacher_proto + (1.0 - momentum) * student_own
    master = lax.all_gather(teacher_proto, "dp", axis=0, tiled=True)
    updated = momentum * master + (1.0 - momentum) * student_proto.astype(jnp.float32)
    updated_unit, updated_inv = unit_columns(updated)
    teacher_half = updated_unit.astype(jnp.bfloat16)
    teacher_logits = jnp.dot(teacher_rows, teacher_half, preferred_element_type=jnp.float32)
    teacher_exp = jnp.exp((teacher_logits - center[None, :]) / teacher_temp)
    student_logits = jnp.dot(student_rows, proto_half, preferred_element_type=jnp.float32)
    student_exp = jnp.exp(student_logits / student_temp)
    teacher_total, student_total = lax.psum(
        (jnp.sum(teacher_exp, axis=1), jnp.sum(student_exp, axis=1)), "fsdp"
    )
    teacher_prob = teacher_exp / teacher_total[:, None]
    student_prob = student_exp / student_total[:, None]
    logit_grads = crop_grads(teacher_prob, student_prob)
    feat_part = jnp.dot(logit_grads, proto_half.T, preferred_element_type=jnp.float32)
    feat_grads = lax.psum(feat_part, "fsdp")
    grad_student_feat = student_inv * (
        feat_grads - student_unit * jnp.sum(student_unit * feat_grads, axis=1, keepdims=True)
    )
    proto_raw = lax.psum_scatter(
        jnp.dot(student_rows.T, logit_grads, preferred_element_type=jnp.float32),
        "dp",
        scatter_dimension=0,
        tiled=True,
    )
    unit_own = lax.dynamic_slice_in_dim(proto_unit, own_start, own_count, 0)
    column_dots = lax.psum(jnp.sum(unit_own * proto_raw, axis=0, keepdims=True), "dp")
    grad_student_proto = proto_inv * (proto_raw - unit_own * column_dots)
    return (new_teacher, grad_student_feat, grad_student_proto)


def solution(mesh):
    placed = (P("dp", "fsdp"), P("dp", "fsdp"), P(None, "fsdp"), P("dp", "fsdp"), P("fsdp"))
    return jax.shard_map(
        body,
        mesh=mesh,
        in_specs=placed,
        out_specs=(P("dp", "fsdp"), P("dp", None), P("dp", "fsdp")),
        check_vma=False,
    )
```

profile of v0, /device:TPU:192, one launch (start us, length us, event | category | flops | bytes accessed | tf_op | source)
XLA Modules:
  0.0 861.7 jit_solution(7654702660854559977)
XLA Ops:
  8.0 96.9 %all-gather = bf16[32,12,768]{2,1,0:T(8,128)(2,1)S(1)} all-gather(bf16[1,12,768]{2,1,0:T(8,128)(2,1)} %bitcast.30), channel_id=1, replica_groups=mesh['dp'=24,'fsdp'=32] {'fsdp'}, dimensions={0}, use_global_device_ids=true | all-gather | bytes 608256 | tf_op jit(solution)/shard_map/all_gather | solution.py:51
  104.8 1.1 reshape.55
  106.0 1.6 copy.10
  107.6 90.8 %all-gather.1 = bf16[32,12,192]{2,1,0:T(8,128)(2,1)S(1)} all-gather(bf16[1,12,192]{2,1,0:T(8,128)(2,1)S(1)} %bitcast.31), channel_id=1, replica_groups=mesh['dp'=24,'fsdp'=32] {'fsdp'}, dimensions={0}, use_global_device_ids=true | all-gather | bytes 152064 | tf_op jit(solution)/shard_map/all_gather | solution.py:52
  198.7 1.4 multiply_reduce_fusion.1
  200.2 2.7 fusion.4
  203.0 4.6 fusion.3
  207.6 2.2 fusion.22
  209.8 85.9 %all-reduce = (f32[192]{0:T(256)S(1)}, f32[768]{0:T(1024)}) all-reduce(f32[192]{0:T(256)S(1)} %get-tuple-element.7, f32[768]{0:T(1024)S(1)} %get-tuple-element.9), channel_id=1, replica_groups=mesh['dp'=24,'fsdp'=32] {'fsdp'}, use_global_device_ids=true, to_apply=%region_7.0 | all-reduce | flops 960 | bytes 7680 | tf_op jit(solution)/shard_map/psum | solution.py:74
  295.7 2.8 broadcast_divide_fusion
  298.5 3.1 reshape.49
  301.6 3.3 reduce_sum.87
  304.9 2.2 broadcast_subtract_fusion
  307.9 5.2 fusion.2
  313.1 1.7 copy-done.2
  314.8 2.8 fusion.14
  317.7 5.1 fusion.21
  324.4 2.1 convert_multiply_fusion.1
  326.5 345.6 %all-reduce.3.cloned.1.call-done = f32[768,384]{1,0:T(8,128)} async-done(((f32[768,384]{1,0:T(8,128)}), f32[768,384]{1,0:T(8,128)}) %all-reduce.3.cloned.1.call-update) | async-done | bytes 1179664 | tf_op jit(solution)/shard_map/psum | solution.py:81
  672.1 1.7 fusion.11
  673.8 1.4 fusion.13
  675.2 122.2 %reduce-scatter.2.cloned.1.call-done = f32[16,2048]{1,0:T(8,128)} async-done(((f32[384,2048]{1,0:T(8,128)}), f32[16,2048]{1,0:T(8,128)}) %reduce-scatter.2.cloned.1.call-update) | async-done | bytes 131088 | tf_op jit(solution)/shard_map/reduce_scatter | solution.py:85
  798.4 55.2 %psum.31 = f32[2048]{0:T(1024)S(1)} all-reduce(f32[2048]{0:T(1024)S(1)} %multiply_reduce_fusion.3), channel_id=1, replica_groups=mesh['dp'=24,'fsdp'=32] {'dp'}, use_global_device_ids=true, to_apply=%region_13.14 | all-reduce | flops 2048 | bytes 16384 | tf_op jit(solution)/shard_map/psum | solution.py:92
  853.6 1.7 subtract_multiply_fusion
  (34 shorter events, 4.5 us)
Async XLA Ops:
  7.2 100.5 %copy-start.6 = (bf16[192,12]{0,1:T(8,128)(2,1)S(1)}, bf16[192,12]{0,1:T(8,128)(2,1)}, u32[]{:S(2)}) copy-start(bf16[192,12]{0,1:T(8,128)(2,1)} %param.6) | copy-start | bytes 13828
  7.2 193.0 %all-gather.4.cloned.1.call-start = ((), (), s32[]{:S(2)}) async-start(), calls=%async_computation.1 | async-start | bytes 3276800 | tf_op jit(solution)/shard_map/all_gather | solution.py:66
  7.9 664.2 %all-reduce.3.cloned.1.call-start = ((), (), s32[]{:S(2)}) async-start(), calls=%async_computation.2 | async-start | bytes 2359296 | tf_op jit(solution)/shard_map/psum | solution.py:81
  104.8 95.3 %copy-start = (bf16[384,2048]{1,0:T(8,128)(2,1)S(1)}, bf16[384,2048]{1,0:T(8,128)(2,1)}, u32[]{:S(2)}) copy-start(bf16[384,2048]{1,0:T(8,128)(2,1)} %param.7) | copy-start | bytes 4718596
  202.9 4.6 copy-start.1
  202.9 4.6 copy-start.5
  307.1 0.8 copy-start.7
  313.1 1.7 copy-start.2
  317.7 479.7 %reduce-scatter.2.cloned.1.call-start = ((), (), s32[]{:S(2)}) async-start(), calls=%async_computation.3 | async-start | bytes 3276800 | tf_op jit(solution)/shard_map/reduce_scatter | solution.py:85
  322.8 0.9 copy-start.4
  672.1 1.7 copy-start.3
Sparse Core Ops, SparseCore 0:
  10.4 128.9 all-gather.3
  317.8 354.2 all-reduce.2
  675.5 121.7 reduce-scatter.1
where the time goes:
time: 862 us
  waiting for transfers between devices  469 us (54%)
  blocking collectives  329 us (38%)
  other arithmetic  26.2 us (3%)
  matrix products  14.7 us (2%)
  between operations  13.9 us (2%)
  local copies, waits for them, and re-layouts  9.38 us (1%)
    psum x1, waiting for transfers between devices, body(): feat_grads = lax.psum(feat_part, 'fsdp')  346 us
    reduce_scatter x1, waiting for transfers between devices, body(): lax.psum_scatter(jnp.dot(student_rows.T, logit_grads, preferred_element_t...  122 us
    all_gather x1, blocking collectives, body(): lax.all_gather(student_feat, 'fsdp', axis=1, tiled=True)  96.9 us
    all_gather x1, blocking collectives, body(): lax.all_gather(teacher_feat, 'fsdp', axis=1, tiled=True)  90.8 us
    psum x1, blocking collectives, body(): lax.psum((jnp.sum(teacher_exp, axis=1), jnp.sum(student_exp, axis=1)), 'f...  85.9 us
    psum x1, blocking collectives, body(): lax.psum(jnp.sum(unit_own * proto_raw, axis=0, keepdims=True), 'dp')  55.2 us
  transfers between devices with their start and end apart: 3, of which 2 were waited for; matrix products, arithmetic and copies ran while one was open for 2% of the time, Pallas kernels for 0%

commit v1 on v0

v1 whole, which is shorter than its diff:
```python
import functools

import jax
import jax.numpy as jnp
from jax import lax
from jax.experimental import pallas as pl
from jax.experimental.pallas import tpu as pltpu
from jax.sharding import PartitionSpec as P

NX, NZL, NC = 4, 3, 2
NY, NZH = 8, 4
STUDENT_CROPS = 8
GLOBAL_CROPS = 2
PROTO = 65536
EPSILON = 1e-06
MOMENTUM = 0.994
TEACHER_TEMP = 0.04
STUDENT_TEMP = 0.1
LANES = 128
COLS = 256
MESH = pl.DeviceIdType.MESH
F32 = jnp.float32
BF16 = jnp.bfloat16


def up(value, unit):
    return -(-value // unit) * unit


def hops(members, odd):
    long, short = members // 2, (members - 1) // 2
    return (short, long) if odd else (long, short)


def kernel(
    pack_ref, proto_ref, teacher_ref, center_ref, feat_ref, raw_ref,
    norm_near, norm_x, feats, masters, half, half_t, proto_inv, unit, rows, rows_t, row_inv,
    t_rows, s_exp, t_exp, s_sum, t_sum, scale, den_y, den_z, grads, feat_sum,
    wire_y, land_y, chunk, wire_z, land_z, final,
    raw, wire_c, land_c, wire_x, land_x, own_x, wire_l, land_l,
    send_sem, recv_sem,
):
    d, f = lax.axis_index("dp"), lax.axis_index("fsdp")
    c, zl, x = lax.rem(d, NC), lax.rem(d // NC, NZL), d // (NC * NZL)
    y, zh = f // NZH, lax.rem(f, NZH)
    bot, count = proto_ref.shape
    s_rows = unit.shape[0]
    t_count = t_rows.shape[0]
    t_pad = up(t_count, LANES)
    width = pack_ref.shape[1]
    tiles = count // COLS

    def at(x_=x, zl_=zl, c_=c, y_=y, zh_=zh):
        return ((x_ * NZL + zl_) * NC + c_, y_ * NZH + zh_)

    def wrap(value, size):
        return lax.rem(value + size, size)

    used = [0]
    started = []

    def send(src, dst, to):
        i = used[0]
        used[0] += 1
        copy = pltpu.make_async_remote_copy(
            src_ref=src, dst_ref=dst, send_sem=send_sem.at[i], recv_sem=recv_sem.at[i],
            device_id=to, device_id_type=MESH,
        )
        copy.start()
        started.append(copy)
        return copy

    near = [
        at(zl_=wrap(zl + k, NZL), c_=lax.rem(c + e, NC))
        for k in range(NZL)
        for e in range(NC)
        if k or e
    ]
    partners = (
        [at(y_=wrap(y + k, NY)) for k in range(1, NY)]
        + [at(zh_=wrap(zh + k, NZH)) for k in range(1, NZH)]
        + near
        + [at(x_=wrap(x + k, NX)) for k in range(1, NX)]
    )
    barrier = pltpu.get_barrier_semaphore()
    for partner in partners:
        pl.semaphore_signal(barrier, inc=1, device_id=partner, device_id_type=MESH)

    feats[y, zh] = pack_ref[...]
    student_own = proto_ref[pl.ds(pl.multiple_of(d * 16, 16), 16), :].astype(F32)
    own_master = MOMENTUM * teacher_ref[...] + (1.0 - MOMENTUM) * student_own
    squares = jnp.sum(own_master * own_master, axis=0, keepdims=True)
    line = lax.broadcasted_iota(jnp.int32, (8, count // 8), 0)
    folded = jnp.zeros((8, count // 8), F32)
    for i in range(8):
        folded = jnp.where(line == i, squares[:, i * (count // 8) : (i + 1) * (count // 8)], folded)
    norm_near[0] = folded
    pl.semaphore_wait(barrier, len(partners))
    norms = [send(norm_near.at[0], norm_near.at[i + 1], to) for i, to in enumerate(near)]

    def gather(buffer, members, spot, ring_to, ring_at, ring_size, direct, others, extra=None):
        came = {}
        for k in range(1, others):
            came[k] = send(spot(0, 0), spot(0, 0), direct(k))
        if extra is not None:
            extra(spot(0, 0))
        right, left = {}, {}
        most = ring_size // 2
        for h in range(1, most + 2):
            for k in range(others):
                r_hops, l_hops = hops(ring_size, k % 2)
                if h == 1 and k > 0:
                    came[k].wait_recv()
                    if extra is not None:
                        extra(spot(0, k))
                if h > 1 and h - 1 <= r_hops:
                    right[k, h - 1].wait_recv()
                    if extra is not None:
                        extra(spot(-(h - 1), k))
                if h <= r_hops:
                    right[k, h] = send(spot(-(h - 1), k), spot(-(h - 1), k), ring_to(1))
                if h > 1 and h - 1 <= l_hops:
                    left[k, h - 1].wait_recv()
                    if extra is not None:
                        extra(spot(h - 1, k))
                if h <= l_hops:
                    left[k, h] = send(spot(h - 1, k), spot(h - 1, k), ring_to(-1))
                yield

    def feat_spot(dy, k):
        return feats.at[wrap(y + dy, NY), wrap(zh - k, NZH)]

    def master_spot(dx, k):
        return masters.at[(wrap(x + dx, NX) * NZL + wrap(zl - k, NZL)) * NC + c]

    across = []

    def to_sibling(block):
        across.append(send(block, block, at(c_=1 - c)))

    feat_steps = gather(
        feats, None, feat_spot, lambda s: at(y_=wrap(y + s, NY)), None, NY,
        lambda k: at(zh_=wrap(zh + k, NZH)), NZH,
    )
    master_steps = gather(
        masters, None, master_spot, lambda s: at(x_=wrap(x + s, NX)), None, NX,
        lambda k: at(zl_=wrap(zl + k, NZL)), NZL, to_sibling,
    )
    next(feat_steps)
    for copy in norms:
        copy.wait_recv()
    norm_x[0] = jnp.sum(norm_near[...], axis=0)
    norms = [send(norm_x.at[0], norm_x.at[k], at(x_=wrap(x + k, NX))) for k in range(1, NX)]
    for k in range(1, NZH):
        next(feat_steps)
    for copy in norms:
        copy.wait_recv()
    inverse = lax.rsqrt(jnp.sum(norm_x[...], axis=0) + EPSILON)
    inverse = jnp.concatenate([inverse[i : i + 1] for i in range(8)], axis=1)
    masters[d] = (own_master * inverse).astype(BF16)
    next(master_steps)

    @pl.loop(0, tiles)
    def _(n):
        at_n = pl.ds(pl.multiple_of(n * COLS, COLS), COLS)
        block = proto_ref[:, at_n].astype(F32)
        inverse = lax.rsqrt(jnp.sum(block * block, axis=0, keepdims=True) + EPSILON)
        normed = block * inverse
        half[:, at_n] = normed.astype(BF16)
        half_t[at_n, :] = normed.T.astype(BF16)
        proto_inv[:, at_n] = inverse

    def drain(*steps):
        live = list(steps)
        while live:
            for one in list(live):
                if next(one, live) is live:
                    live.remove(one)

    drain(feat_steps, master_steps)
    for copy in across:
        copy.wait_recv()

    slots = feats[...].reshape(NY * NZH * 16, width)
    spots = lax.broadcasted_iota(jnp.int32, (bot, NY * NZH * 16), 1)
    wanted = lax.broadcasted_iota(jnp.int32, (bot, NY * NZH * 16), 0)
    owner = lax.shift_right_logical(wanted * 5462, 16)
    pick_s = (spots == owner * 16 + (wanted - owner * 12)).astype(F32).astype(BF16)
    pick_t = (spots == owner * 16 + 12 + (wanted & 3)).astype(F32).astype(BF16)
    student_t = jnp.dot(pick_s, slots[:, :s_rows], preferred_element_type=F32)
    inverse = lax.rsqrt(jnp.sum(student_t * student_t, axis=0, keepdims=True) + EPSILON)
    rows_t[...] = (student_t * inverse).astype(BF16)
    student = student_t.T
    inverse = lax.rsqrt(jnp.sum(student * student, axis=1, keepdims=True) + EPSILON)
    normed = student * inverse
    unit[...] = normed
    rows[...] = normed.astype(BF16)
    row_inv[...] = jnp.broadcast_to(inverse, row_inv.shape)
    pieces = jnp.dot(pick_t, slots[:, : 3 * t_pad], preferred_element_type=F32)
    place = lax.broadcasted_iota(jnp.int32, (bot, t_pad), 0)
    owner = lax.shift_right_logical(place * 5462, 16)
    quarter = lax.shift_right_logical(place - owner * 12, 2)
    teacher_t = jnp.where(
        quarter == 0,
        pieces[:, :t_pad],
        jnp.where(quarter == 1, pieces[:, t_pad : 2 * t_pad], pieces[:, 2 * t_pad :]),
    )
    teacher = teacher_t.T[:t_count]
    inverse = lax.rsqrt(jnp.sum(teacher * teacher, axis=1, keepdims=True) + EPSILON)
    t_rows[...] = (teacher * inverse).astype(BF16)

    def fold(values):
        return values[:, :LANES] + values[:, LANES:]

    s_sum[...] = jnp.zeros_like(s_sum)
    t_sum[...] = jnp.zeros_like(t_sum)

    @pl.loop(0, tiles)
    def _(n):
        at_n = pl.ds(pl.multiple_of(n * COLS, COLS), COLS)
        block = masters[:, :, at_n].reshape(bot, COLS)
        logits = jnp.dot(t_rows[...], block, preferred_element_type=F32)
        value = jnp.exp((logits - center_ref[:, at_n]) * (1.0 / TEACHER_TEMP))
        t_exp[:, at_n] = value
        t_sum[:t_count, :] += fold(value)

    @pl.loop(0, tiles)
    def _(n):
        at_n = pl.ds(pl.multiple_of(n * COLS, COLS), COLS)
        logits = jnp.dot(rows[...], half[:, at_n], preferred_element_type=F32)
        value = jnp.exp(logits * (1.0 / STUDENT_TEMP))
        s_exp[:, at_n] = value
        s_sum[:s_rows, :] += fold(value)

    s_tiles, t_tiles = s_sum.shape[0] // LANES, t_sum.shape[0] // LANES
    line = lax.broadcasted_iota(jnp.int32, (8, LANES), 0)
    lane = lax.broadcasted_iota(jnp.int32, (8, LANES), 1)
    packed = jnp.zeros((8, LANES), F32)
    for i in range(s_tiles + t_tiles):
        block = (
            s_sum[i * LANES : (i + 1) * LANES, :]
            if i < s_tiles
            else t_sum[(i - s_tiles) * LANES : (i - s_tiles + 1) * LANES, :]
        )
        packed = jnp.where(line == i, jnp.sum(block.T, axis=0, keepdims=True), packed)
    den_y[0] = packed
    met = [send(den_y.at[0], den_y.at[k], at(y_=wrap(y + k, NY))) for k in range(1, NY)]
    for copy in met:
        copy.wait_recv()
    den_z[0] = jnp.sum(den_y[...], axis=0)
    met = [send(den_z.at[0], den_z.at[k], at(zh_=wrap(zh + k, NZH))) for k in range(1, NZH)]
    for copy in met:
        copy.wait_recv()
    total = jnp.sum(den_z[...], axis=0)
    inverse = (PROTO / 16.0 / STUDENT_TEMP) / jnp.where(total > 0.0, total, 1.0)
    crop = lax.broadcasted_iota(jnp.int32, (LANES, LANES), 0) & (STUDENT_CROPS - 1)
    copies = jnp.where(crop < GLOBAL_CROPS, F32(GLOBAL_CROPS - 1), F32(GLOBAL_CROPS))
    for i in range(s_tiles + t_tiles):
        block = jnp.broadcast_to(inverse[i : i + 1, :], (LANES, LANES)).T
        scale[i * LANES : (i + 1) * LANES, :] = block * copies if i < s_tiles else block

    position = lax.broadcasted_iota(jnp.int32, (STUDENT_CROPS, count), 0)
    group = 4

    @pl.loop(0, t_count // (GLOBAL_CROPS * group))
    def _(i):
        at_t = pl.ds(pl.multiple_of(i * 8, 8), 8)
        at_s = pl.ds(pl.multiple_of(i * 32, 32), 32)
        t_scale = scale[pl.ds(pl.multiple_of(s_tiles * LANES + i * 8, 8), 8), :1]
        prob = t_exp[at_t, :] * t_scale
        value = s_exp[at_s, :] * scale[at_s, :1]
        out = []
        for a in range(group):
            first, second = prob[2 * a : 2 * a + 1], prob[2 * a + 1 : 2 * a + 2]
            partner = jnp.where(
                position == 0, second, jnp.where(position == 1, first, first + second)
            )
            out.append(value[8 * a : 8 * a + 8] - partner)
        grads[at_s, :] = jnp.concatenate(out, axis=0).astype(BF16)

    deep = 512 if count % 512 == 0 else COLS
    feat_sum[...] = jnp.zeros_like(feat_sum)

    @pl.loop(0, count // deep)
    def _(n):
        at_n = pl.ds(pl.multiple_of(n * deep, deep), deep)
        feat_sum[...] += jnp.dot(grads[:, at_n], half_t[at_n, :], preferred_element_type=F32)

    part = feat_sum[...]
    along = jnp.sum(unit[...] * part, axis=1, keepdims=True)
    feat_sum[...] = row_inv[:, :1] * (part - unit[...] * along)

    y_rows = s_rows // NY
    r_hops, l_hops = hops(NY, 0)

    def own_y(j):
        return feat_sum[pl.ds(pl.multiple_of(j * y_rows, 8), y_rows), :]

    def reduce_y():
        right, left = {}, {}
        for h in range(1, r_hops + 1):
            value = own_y(wrap(y + (r_hops + 1 - h), NY))
            if h > 1:
                right[h - 1].wait_recv()
                value = value + land_y[0, h - 2].astype(F32)
            wire_y[0, h - 1] = value.astype(BF16)
            right[h] = send(wire_y.at[0, h - 1], land_y.at[0, h - 1], at(y_=wrap(y + 1, NY)))
            if h <= l_hops:
                value = own_y(wrap(y - (l_hops + 1 - h), NY))
                if h > 1:
                    left[h - 1].wait_recv()
                    value = value + land_y[1, h - 2].astype(F32)
                wire_y[1, h - 1] = value.astype(BF16)
                left[h] = send(wire_y.at[1, h - 1], land_y.at[1, h - 1], at(y_=wrap(y - 1, NY)))
            yield
        value = own_y(y)
        if l_hops:
            left[l_hops].wait_recv()
            value = value + land_y[1, l_hops - 1].astype(F32)
        right[r_hops].wait_recv()
        value = value + land_y[0, r_hops - 1].astype(F32)
        chunk[...] = value.reshape(chunk.shape)
        met = []
        for k in range(1, NZH):
            wire_z[k] = chunk[wrap(zh + k, NZH)].astype(BF16)
            met.append(send(wire_z.at[k], land_z.at[k], at(zh_=wrap(zh + k, NZH))))
        yield
        value = chunk[zh]
        for k in range(1, NZH):
            met[k - 1].wait_recv()
            value = value + land_z[k].astype(F32)
        final[y, zh] = value.astype(BF16)
        yield from gather(
            final, None, lambda dy, k: final.at[wrap(y + dy, NY), wrap(zh - k, NZH)],
            lambda s: at(y_=wrap(y + s, NY)), None, NY,
            lambda k: at(zh_=wrap(zh + k, NZH)), NZH,
        )

    tail = reduce_y()
    next(tail)

    @pl.loop(0, tiles)
    def _(n):
        at_n = pl.ds(pl.multiple_of(n * COLS, COLS), COLS)
        part = jnp.dot(rows_t[...], grads[:, at_n], preferred_element_type=F32)
        inverse = proto_inv[:, at_n]
        normed = proto_ref[:, at_n].astype(F32) * inverse
        along = jnp.sum(normed * part, axis=0, keepdims=True)
        part = inverse * (part - normed * along)
        raw[:, :, :, at_n] = part.reshape(NX * NZL, NC, 16, COLS)
        wire_c[:, :, at_n] = raw[:, pl.ds(1 - c, 1), :, at_n].reshape(NX * NZL, 16, COLS).astype(BF16)

    def reduce_x():
        over = {}
        for k in range(NX):
            block = wrap(x + (NX // 2 + 2 * NX - k), 2 * NX)
            block = lax.rem(block, NX)
            at_k = pl.ds(block * NZL, NZL)
            over[NX // 2 - k] = send(wire_c.at[at_k], land_c.at[at_k], at(c_=1 - c))
        for copy in over.values():
            copy.wait_recv()

        def own(dx, k):
            slot = wrap(x + dx, NX) * NZL + k
            return raw[slot, c] + land_c[slot].astype(F32)

        right, left = {}, {}
        for h in range(1, NX // 2 + 1):
            for k in range(NZL):
                r_hops, l_hops = hops(NX, k % 2)
                if h <= r_hops:
                    value = own(r_hops + 1 - h, k)
                    if h > 1:
                        right[k, h - 1].wait_recv()
                        value = value + land_x[0, k, h - 2].astype(F32)
                    wire_x[0, k, h - 1] = value.astype(BF16)
                    right[k, h] = send(
                        wire_x.at[0, k, h - 1], land_x.at[0, k, h - 1], at(x_=wrap(x + 1, NX))
                    )
                if h <= l_hops:
                    value = own(-(l_hops + 1 - h), k)
                    if h > 1:
                        left[k, h - 1].wait_recv()
                        value = value + land_x[1, k, h - 2].astype(F32)
                    wire_x[1, k, h - 1] = value.astype(BF16)
                    left[k, h] = send(
                        wire_x.at[1, k, h - 1], land_x.at[1, k, h - 1], at(x_=wrap(x - 1, NX))
                    )
                yield
        for k in range(NZL):
            r_hops, l_hops = hops(NX, k % 2)
            value = own(0, k)
            if l_hops:
                left[k, l_hops].wait_recv()
                value = value + land_x[1, k, l_hops - 1].astype(F32)
            if r_hops:
                right[k, r_hops].wait_recv()
                value = value + land_x[0, k, r_hops - 1].astype(F32)
            own_x[k] = value
        met = []
        for k in range(1, NZL):
            wire_l[k] = own_x[wrap(zl + k, NZL)].astype(BF16)
            met.append(send(wire_l.at[k], land_l.at[k], at(zl_=wrap(zl + k, NZL))))
        yield
        value = own_x[zl]
        for k in range(1, NZL):
            met[k - 1].wait_recv()
            value = value + land_l[k].astype(F32)
        raw_ref[...] = value

    drain(tail, reduce_x())
    for i in range(NY):
        feat_ref[i * y_rows : (i + 1) * y_rows, :] = (
            final[i].astype(F32).reshape(y_rows, bot).astype(BF16)
        )

    for copy in started:
        copy.wait_send()


def call(pack, proto, teacher, center, s_rows, t_rows):
    bot, count = proto.shape
    y_rows = s_rows // NY
    z_rows = y_rows // NZH
    width = pack.shape[1]
    vmem = pltpu.VMEM
    ring, short = NY // 2, NX // 2
    s_pad, t_pad = up(s_rows, LANES), up(t_rows, LANES)
    copies = (
        (NZL * NC - 1) + (NX - 1) + (NZH - 1) + NZH * (NY - 1)
        + (NZL - 1) + NZL * (NX - 1) + NZL * NX
        + (NY - 1) + (NZH - 1)
        + (NY - 1) + (NZH - 1) + (NZH - 1) + NZH * (NY - 1)
        + NX + NZL * (NX - 1) + (NZL - 1)
    )
    return pl.pallas_call(
        kernel,
        out_shape=(
            jax.ShapeDtypeStruct((s_rows, bot), BF16),
            jax.ShapeDtypeStruct((16, count), F32),
        ),
        in_specs=[pl.BlockSpec(memory_space=pltpu.VMEM)] * 4,
        out_specs=[pl.BlockSpec(memory_space=pltpu.VMEM)] * 2,
        scratch_shapes=[
            vmem((NZL * NC, 8, count // 8), F32),
            vmem((NX, 8, count // 8), F32),
            vmem((NY, NZH, 16, width), BF16),
            vmem((NX * NZL * NC, 16, count), BF16),
            vmem((bot, count), BF16),
            vmem((count, bot), BF16),
            vmem((1, count), F32),
            vmem((s_rows, bot), F32),
            vmem((s_rows, bot), BF16),
            vmem((bot, s_rows), BF16),
            vmem((s_rows, LANES), F32),
            vmem((t_rows, bot), BF16),
            vmem((s_rows, count), F32),
            vmem((t_rows, count), F32),
            vmem((s_pad, LANES), F32),
            vmem((t_pad, LANES), F32),
            vmem((s_pad + t_pad, LANES), F32),
            vmem((NY, 8, LANES), F32),
            vmem((NZH, 8, LANES), F32),
            vmem((s_rows, count), BF16),
            vmem((s_rows, bot), F32),
            vmem((2, ring, y_rows, bot), BF16),
            vmem((2, ring, y_rows, bot), BF16),
            vmem((NZH, z_rows, bot), F32),
            vmem((NZH, z_rows, bot), BF16),
            vmem((NZH, z_rows, bot), BF16),
            vmem((NY, NZH, z_rows, bot), BF16),
            vmem((NX * NZL, NC, 16, count), F32),
            vmem((NX * NZL, 16, count), BF16),
            vmem((NX * NZL, 16, count), BF16),
            vmem((2, NZL, short, 16, count), BF16),
            vmem((2, NZL, short, 16, count), BF16),
            vmem((NZL, 16, count), F32),
            vmem((NZL, 16, count), BF16),
            vmem((NZL, 16, count), BF16),
            pltpu.SemaphoreType.DMA((copies,)),
            pltpu.SemaphoreType.DMA((copies,)),
        ],
        compiler_params=pltpu.CompilerParams(
            collective_id=0, has_side_effects=True, vmem_limit_bytes=56 * 1024 * 1024
        ),
    )(pack, proto, teacher, center)


def body(student_feat, teacher_feat, student_proto, teacher_proto, center):
    s_rows, t_rows = student_feat.shape[0], teacher_feat.shape[0]
    t_pad = up(t_rows, LANES)
    width = max(s_rows, 3 * t_pad)
    student_t, teacher_t = student_feat.T, teacher_feat.T
    pieces = [jnp.pad(teacher_t[4 * q : 4 * q + 4], ((0, 0), (0, t_pad - t_rows))) for q in range(3)]
    pieces = jnp.concatenate(pieces, axis=1)
    pack = jnp.concatenate(
        [
            jnp.pad(student_t, ((0, 0), (0, width - s_rows))),
            jnp.pad(pieces, ((0, 0), (0, width - 3 * t_pad))),
        ],
        axis=0,
    )
    own_count = teacher_proto.shape[0]
    student_own = lax.dynamic_slice_in_dim(
        student_proto, lax.axis_index("dp") * own_count, own_count, 0
    ).astype(F32)
    new_teacher = MOMENTUM * teacher_proto + (1.0 - MOMENTUM) * student_own
    feat, raw = call(pack, student_proto, teacher_proto, center.reshape(1, -1), s_rows, t_rows)
    return (new_teacher, feat.astype(F32), raw)


def solution(mesh):
    placed = (P("dp", "fsdp"), P("dp", "fsdp"), P(None, "fsdp"), P("dp", "fsdp"), P("fsdp"))
    return jax.shard_map(
        body,
        mesh=mesh,
        in_specs=placed,
        out_specs=(P("dp", "fsdp"), P("dp", None), P("dp", "fsdp")),
        check_vma=False,
    )
```

time: 862 us -> 123 us (0.14)
  the two profiles are of different devices: /device:TPU:192 before, /device:TPU:16 now
where the time goes in v1:
time: 123 us
  Pallas kernels  115 us (93%)
  other arithmetic  5.06 us (4%)
  local copies, waits for them, and re-layouts  1.43 us (1%)
    pallas_call x1, Pallas kernels, call(): pl.pallas_call(kernel, out_shape=(jax.ShapeDtypeStruct((s_rows, bot), BF1...  115 us

profile of v1, /device:TPU:16, one launch (start us, length us, event | category | flops | bytes accessed | tf_op | source)
XLA Modules:
  0.0 122.6 jit_solution(14918728908333645591)
XLA Ops:
  0.6 0.8 fusion.13
  1.4 1.4 %fusion.11.pack_ref = bf16[16,768]{1,0:T(8,128)(2,1)} fusion(bf16[4,192]{1,0:T(4,128)(2,1)S(1)} %get-tuple-element.8, bf16[4,192]{1,0:T(4,128)(2,1)S(1)} %get-tuple-element.9, bf16[4,192]{1,0:T(4,128)(2,1)S(1)} %get-tuple-element.7, bf16[12,768]{1,0:T(8,128)(2,1)} %bitcast.3), kind=kLoop, calls=%fused_computation.17 | loop fusion | flops 282624 | bytes 47616 | tf_op jit(solution)/shard_map/concatenate | solution.py:496
  2.8 0.0 copy-start
  2.8 115.5 %shard_map.76 = (bf16[768,384]{1,0:T(8,128)(2,1)}, f32[16,2048]{1,0:T(8,128)}) custom-call(bf16[16,768]{1,0:T(8,128)(2,1)} %fusion.11.pack_ref, bf16[384,2048]{1,0:T(8,128)(2,1)} %proto_ref.1, f32[16,2048]{1,0:T(8,128)} %teacher_ref.1, f32[1,2048]{1,0:T(1,128)} %bitcast.4), custom_call_target="tpu_custom_call" | custom-call | tf_op jit(solution)/shard_map/pallas_call | solution.py:436
  118.2 0.0 copy-start.1
  118.2 2.2 %convert_element_type.11 = f32[768,384]{1,0:T(8,128)} convert(bf16[768,384]{1,0:T(8,128)(2,1)} %get-tuple-element.5) | non-fusion elementwise | flops 294912 | bytes 1769472 | tf_op jit(solution)/shard_map/convert_element_type | solution.py:509
  120.4 0.0 copy-done
  120.4 1.5 %multiply_add_fusion = f32[16,2048]{1,0:T(8,128)} fusion(f32[16,2048]{1,0:T(8,128)S(1)} %copy-done, bf16[384,2048]{1,0:T(8,128)(2,1)} %proto_ref.1, s32[]{:T(128)S(6)} %select_n.3), kind=kLoop, calls=%fused_computation | loop fusion | flops 131072 | bytes 327684 | tf_op jit(solution)/shard_map/add | solution.py:507
  121.9 0.0 copy-done.1
  121.9 0.7 copy.9
Async XLA Ops:
  2.8 117.7 %copy-start = (f32[16,2048]{1,0:T(8,128)S(1)}, f32[16,2048]{1,0:T(8,128)}, u32[]{:S(2)}) copy-start(f32[16,2048]{1,0:T(8,128)} %teacher_ref.1) | copy-start | bytes 393220
  118.2 3.7 %copy-start.1 = (f32[16,2048]{1,0:T(8,128)S(1)}, f32[16,2048]{1,0:T(8,128)}, u32[]{:S(2)}) copy-start(f32[16,2048]{1,0:T(8,128)} %get-tuple-element.15) | copy-start | bytes 393220

commit v2 on v1

v2 whole, which is shorter than its diff:
```python
import functools

import jax
import jax.numpy as jnp
from jax import lax
from jax.experimental import pallas as pl
from jax.experimental.pallas import tpu as pltpu
from jax.sharding import PartitionSpec as P

NX, NZL, NC = 4, 3, 2
NY, NZH = 8, 4
STUDENT_CROPS = 8
GLOBAL_CROPS = 2
PROTO = 65536
EPSILON = 1e-06
MOMENTUM = 0.994
TEACHER_TEMP = 0.04
STUDENT_TEMP = 0.1
LANES = 128
COLS = 256
MESH = pl.DeviceIdType.MESH
F32 = jnp.float32
BF16 = jnp.bfloat16


def up(value, unit):
    return -(-value // unit) * unit


def hops(members, odd):
    long, short = members // 2, (members - 1) // 2
    return (short, long) if odd else (long, short)


class Spread:
    def __init__(self, send, spot, to, size, odd):
        self.send, self.spot, self.to = send, spot, to
        self.reach = dict(zip((1, -1), hops(size, odd)))
        self.out = {}

    def first(self):
        for way in (1, -1):
            for s in range(min(2, self.reach[way]), 0, -1):
                self.out[way, s] = self.send(self.spot(0), self.spot(0), self.to(way * s))

    def second(self):
        for way in (1, -1):
            if self.reach[way] > 2:
                self.out[way, 2].wait_recv()
                block = self.spot(-2 * way)
                for s in range(self.reach[way] - 2, 0, -1):
                    self.out[way, s + 2] = self.send(block, block, self.to(way * s))

    def arrivals(self):
        for way in (1, -1):
            for s in range(1, self.reach[way] + 1):
                if not (s == 2 and self.reach[way] > 2):
                    yield self.out[way, s], self.spot(-way * s)

    def last(self):
        for copy, _ in self.arrivals():
            copy.wait_recv()


class Gathered:
    def __init__(self, send, own, wire, land, to, size, odd):
        self.send, self.own, self.wire, self.land, self.to = send, own, wire, land, to
        self.reach = dict(zip((1, -1), hops(size, odd)))
        self.out = {}

    def post(self, way, kind, value, steps):
        side = 0 if way == 1 else 1
        self.wire[side, kind] = value.astype(self.wire.dtype)
        self.out[way, kind] = self.send(
            self.wire.at[side, kind], self.land.at[side, kind], self.to(way * steps)
        )

    def took(self, way, kind):
        self.out[way, kind].wait_recv()
        return self.land[0 if way == 1 else 1, kind].astype(F32)

    def first(self):
        for way in (1, -1):
            if self.reach[way] > 3:
                self.post(way, 3, self.own(4 * way), 2)
        for way in (1, -1):
            if self.reach[way] > 2:
                self.post(way, 2, self.own(3 * way), 1)
        for way in (1, -1):
            if self.reach[way] > 0:
                self.post(way, 0, self.own(way), 1)

    def second(self):
        for way in (1, -1):
            if self.reach[way] > 1:
                value = self.own(2 * way)
                for kind in (2, 3):
                    if self.reach[way] > kind:
                        value = value + self.took(way, kind)
                self.post(way, 1, value, 2)

    def total(self):
        value = self.own(0)
        for kind in (0, 1):
            for way in (1, -1):
                if self.reach[way] > kind:
                    value = value + self.took(way, kind)
        return value


def kernel(
    pack_ref, proto_ref, teacher_ref, center_ref, new_ref, feat_ref, raw_ref,
    norm_near, norm_x, feats, masters, half, half_t, proto_inv, unit, rows, rows_t, row_inv,
    t_rows, s_exp, t_exp, s_sum, t_sum, scale, den_y, den_z, grads, s_part, t_part,
    s_wire, s_land, t_wire, t_land, s_chunk, s_wire_z, s_land_z, t_chunk, t_land_z, final,
    raw, wire_c, land_c, wire_x, land_x, own_x, wire_l, land_l,
    send_sem, recv_sem,
):
    d, f = lax.axis_index("dp"), lax.axis_index("fsdp")
    c, zl, x = lax.rem(d, NC), lax.rem(d // NC, NZL), d // (NC * NZL)
    y, zh = f // NZH, lax.rem(f, NZH)
    bot, count = proto_ref.shape
    s_rows = unit.shape[0]
    t_pad = t_sum.shape[0]
    width = pack_ref.shape[1]
    tiles = count // COLS
    s_tiles, t_tiles = s_sum.shape[0] // LANES, t_pad // LANES
    share = s_rows // (NY * NZH)
    images = share // STUDENT_CROPS
    t_used = NY * NZH * 8

    def at(x_=x, zl_=zl, c_=c, y_=y, zh_=zh):
        return ((x_ * NZL + zl_) * NC + c_, y_ * NZH + zh_)

    def wrap(value, size):
        return lax.rem(value + size, size)

    def to_y(s):
        return at(y_=wrap(y + s, NY))

    def to_x(s):
        return at(x_=wrap(x + s, NX))

    def to_zh(k):
        return at(zh_=wrap(zh + k, NZH))

    def to_zl(k):
        return at(zl_=wrap(zl + k, NZL))

    used = [0]
    started = []

    def send(src, dst, to):
        i = used[0]
        used[0] += 1
        copy = pltpu.make_async_remote_copy(
            src_ref=src, dst_ref=dst, send_sem=send_sem.at[i], recv_sem=recv_sem.at[i],
            device_id=to, device_id_type=MESH,
        )
        copy.start()
        started.append(copy)
        return copy

    near = [
        at(zl_=wrap(zl + k, NZL), c_=lax.rem(c + e, NC))
        for k in range(NZL)
        for e in range(NC)
        if k or e
    ]
    partners = (
        [to_y(k) for k in range(1, NY)]
        + [to_zh(k) for k in range(1, NZH)]
        + near
        + [to_x(k) for k in range(1, NX)]
    )
    barrier = pltpu.get_barrier_semaphore()
    for partner in partners:
        pl.semaphore_signal(barrier, inc=1, device_id=partner, device_id_type=MESH)

    feats[y, zh] = pack_ref[...]
    student_own = proto_ref[pl.ds(pl.multiple_of(d * 16, 16), 16), :].astype(F32)
    own_master = MOMENTUM * teacher_ref[...] + (1.0 - MOMENTUM) * student_own
    new_ref[...] = own_master
    squares = jnp.sum(own_master * own_master, axis=0, keepdims=True)
    line = lax.broadcasted_iota(jnp.int32, (8, count // 8), 0)
    folded = jnp.zeros((8, count // 8), F32)
    for i in range(8):
        folded = jnp.where(line == i, squares[:, i * (count // 8) : (i + 1) * (count // 8)], folded)
    norm_near[0] = folded
    pl.semaphore_wait(barrier, len(partners))
    norms = [send(norm_near.at[0], norm_near.at[i + 1], to) for i, to in enumerate(near)]

    def along_z(buffer):
        return [send(buffer.at[y, zh], buffer.at[y, zh], to_zh(k)) for k in range(1, NZH)]

    def along_y(buffer):
        def spot_of(k):
            return lambda dy: buffer.at[wrap(y + dy, NY), wrap(zh - k, NZH)]

        return [Spread(send, spot_of(k), to_y, NY, k % 2) for k in range(NZH)]

    order = sorted(range(1, NZH), key=lambda k: (min(k, NZH - k), k))
    feat_z = along_z(feats)
    feat_y = along_y(feats)
    feat_y[0].first()

    @pl.loop(0, tiles)
    def _(n):
        at_n = pl.ds(pl.multiple_of(n * COLS, COLS), COLS)
        block = proto_ref[:, at_n].astype(F32)
        inverse = lax.rsqrt(jnp.sum(block * block, axis=0, keepdims=True) + EPSILON)
        normed = block * inverse
        half[:, at_n] = normed.astype(BF16)
        half_t[at_n, :] = normed.T.astype(BF16)
        proto_inv[:, at_n] = inverse

    for copy in norms:
        copy.wait_recv()
    norm_x[0] = jnp.sum(norm_near[...], axis=0)
    norms = [send(norm_x.at[0], norm_x.at[k], to_x(k)) for k in range(1, NX)]
    feat_y[0].second()
    for k in order:
        feat_z[k - 1].wait_recv()
        feat_y[k].first()
    for copy in norms:
        copy.wait_recv()
    inverse = lax.rsqrt(jnp.sum(norm_x[...], axis=0) + EPSILON)
    inverse = jnp.concatenate([inverse[i : i + 1] for i in range(8)], axis=1)
    masters[d] = (own_master * inverse).astype(BF16)

    across = []

    def to_sibling(block):
        across.append(send(block, block, at(c_=1 - c)))

    def master_of(k):
        return lambda dx: masters.at[(wrap(x + dx, NX) * NZL + wrap(zl - k, NZL)) * NC + c]

    master_z = [send(masters.at[d], masters.at[d], to_zl(k)) for k in range(1, NZL)]
    master_x = [Spread(send, master_of(k), to_x, NX, k % 2) for k in range(NZL)]
    master_x[0].first()
    to_sibling(masters.at[d])
    for k in order:
        feat_y[k].second()
    for k in range(1, NZL):
        master_z[k - 1].wait_recv()
        master_x[k].first()
        to_sibling(master_of(k)(0))
    for one in feat_y:
        one.last()
    for copy, block in master_x[0].arrivals():
        copy.wait_recv()
        to_sibling(block)

    slots = feats[...].reshape(NY * NZH * 16, width)
    spots = lax.broadcasted_iota(jnp.int32, (bot, NY * NZH * 16), 1)
    wanted = lax.broadcasted_iota(jnp.int32, (bot, NY * NZH * 16), 0)
    owner = lax.shift_right_logical(wanted * 5462, 16)
    pick_s = (spots == owner * 16 + (wanted - owner * 12)).astype(F32).astype(BF16)
    pick_t = (spots == owner * 16 + 12 + (wanted & 3)).astype(F32).astype(BF16)
    student_t = jnp.dot(pick_s, slots[:, :s_rows], preferred_element_type=F32)
    inverse = lax.rsqrt(jnp.sum(student_t * student_t, axis=0, keepdims=True) + EPSILON)
    rows_t[...] = (student_t * inverse).astype(BF16)
    student = student_t.T
    inverse = lax.rsqrt(jnp.sum(student * student, axis=1, keepdims=True) + EPSILON)
    normed = student * inverse
    unit[...] = normed
    rows[...] = normed.astype(BF16)
    row_inv[...] = jnp.broadcast_to(inverse, row_inv.shape)
    pieces = jnp.dot(pick_t, slots[:, : 3 * t_pad], preferred_element_type=F32)
    place = lax.broadcasted_iota(jnp.int32, (bot, t_pad), 0)
    owner = lax.shift_right_logical(place * 5462, 16)
    quarter = lax.shift_right_logical(place - owner * 12, 2)
    teacher_t = jnp.where(
        quarter == 0,
        pieces[:, :t_pad],
        jnp.where(quarter == 1, pieces[:, t_pad : 2 * t_pad], pieces[:, 2 * t_pad :]),
    )
    teacher = teacher_t.T
    inverse = lax.rsqrt(jnp.sum(teacher * teacher, axis=1, keepdims=True) + EPSILON)
    to_row = lax.broadcasted_iota(jnp.int32, (t_pad, t_pad), 0)
    from_row = lax.broadcasted_iota(jnp.int32, (t_pad, t_pad), 1)
    place = to_row & 7
    moved = (from_row == lax.shift_right_logical(to_row, 3) * (2 * images) + place) & (place < 2 * images)
    t_rows[...] = jnp.dot(
        moved.astype(F32).astype(BF16), (teacher * inverse).astype(BF16), preferred_element_type=F32
    ).astype(BF16)

    def fold(values):
        return values[:, :LANES] + values[:, LANES:]

    s_sum[...] = jnp.zeros_like(s_sum)
    t_sum[...] = jnp.zeros_like(t_sum)
    s_part[...] = jnp.zeros_like(s_part)
    t_part[...] = jnp.zeros_like(t_part)

    @pl.loop(0, tiles)
    def _(n):
        at_n = pl.ds(pl.multiple_of(n * COLS, COLS), COLS)
        logits = jnp.dot(rows[...], half[:, at_n], preferred_element_type=F32)
        value = jnp.exp(logits * (1.0 / STUDENT_TEMP))
        s_exp[:, at_n] = value
        s_sum[:s_rows, :] += fold(value)
        s_part[...] += jnp.dot(value.astype(BF16), half_t[at_n, :], preferred_element_type=F32)

    part = s_part[...]
    s_part[...] = part - unit[...] * jnp.sum(unit[...] * part, axis=1, keepdims=True)

    y_rows = s_rows // NY
    piece = y_rows // 2

    def own_s(h):
        def own(dy):
            start = wrap(y + dy, NY) * y_rows + h * piece
            return s_part[pl.ds(pl.multiple_of(start, 8), piece), :]

        return own

    s_ring = [
        Gathered(send, own_s(h), s_wire.at[h], s_land.at[h], to_y, NY, h) for h in range(2)
    ]
    for one in s_ring:
        one.first()
    for k in range(1, NZL):
        for copy, block in master_x[k].arrivals():
            copy.wait_recv()
            to_sibling(block)
    for copy in across:
        copy.wait_recv()

    @pl.loop(0, tiles)
    def _(n):
        at_n = pl.ds(pl.multiple_of(n * COLS, COLS), COLS)
        block = masters[:, :, at_n].reshape(bot, COLS)
        logits = jnp.dot(t_rows[...], block, preferred_element_type=F32)
        value = jnp.exp((logits - center_ref[:, at_n]) * (1.0 / TEACHER_TEMP))
        t_exp[:, at_n] = value
        t_sum[...] += fold(value)
        t_part[...] += jnp.dot(value.astype(BF16), half_t[at_n, :], preferred_element_type=F32)

    def own_t(dy):
        return t_part[pl.ds(pl.multiple_of(wrap(y + dy, NY) * (8 * NZH), 8), 8 * NZH), :]

    t_ring = Gathered(send, own_t, t_wire, t_land, to_y, NY, 1)
    t_ring.first()
    line = lax.broadcasted_iota(jnp.int32, (8, LANES), 0)
    packed = jnp.zeros((8, LANES), F32)
    for i in range(s_tiles + t_tiles):
        block = (
            s_sum[i * LANES : (i + 1) * LANES, :]
            if i < s_tiles
            else t_sum[(i - s_tiles) * LANES : (i - s_tiles + 1) * LANES, :]
        )
        packed = jnp.where(line == i, jnp.sum(block.T, axis=0, keepdims=True), packed)
    den_y[0] = packed
    dens = [send(den_y.at[0], den_y.at[k], to_y(k)) for k in range(1, NY)]
    for one in s_ring:
        one.second()
    t_ring.second()
    for copy in dens:
        copy.wait_recv()
    den_z[0] = jnp.sum(den_y[...], axis=0)
    dens = [send(den_z.at[0], den_z.at[k], to_zh(k)) for k in range(1, NZH)]
    s_chunk[...] = jnp.concatenate([one.total() for one in s_ring], axis=0).reshape(s_chunk.shape)
    s_met = []
    for k in range(1, NZH):
        s_wire_z[k] = s_chunk[wrap(zh + k, NZH)].astype(BF16)
        s_met.append(send(s_wire_z.at[k], s_land_z.at[k], to_zh(k)))
    t_chunk[...] = t_ring.total().reshape(t_chunk.shape)
    t_met = [
        send(t_chunk.at[wrap(zh + k, NZH)], t_land_z.at[k], to_zh(k)) for k in range(1, NZH)
    ]
    for copy in dens:
        copy.wait_recv()
    total = jnp.sum(den_z[...], axis=0)
    inverse = (PROTO / 16.0 / STUDENT_TEMP) / jnp.where(total > 0.0, total, 1.0)
    crop = lax.broadcasted_iota(jnp.int32, (LANES, LANES), 0) & (STUDENT_CROPS - 1)
    copies = jnp.where(crop < GLOBAL_CROPS, F32(GLOBAL_CROPS - 1), F32(GLOBAL_CROPS))
    for i in range(s_tiles + t_tiles):
        block = jnp.broadcast_to(inverse[i : i + 1, :], (LANES, LANES)).T
        scale[i * LANES : (i + 1) * LANES, :] = block * copies if i < s_tiles else block

    def partner_of(prob, i, position):
        first, second = prob[2 * i : 2 * i + 1], prob[2 * i + 1 : 2 * i + 2]
        return jnp.where(position == 0, second, jnp.where(position == 1, first, first + second))

    position = lax.broadcasted_iota(jnp.int32, (STUDENT_CROPS, count), 0)

    @pl.loop(0, NY * NZH // 2)
    def _(i):
        out = []
        for e in range(2):
            g = i * 2 + e
            at_t = pl.ds(pl.multiple_of(g * 8, 8), 8)
            at_s = pl.ds(pl.multiple_of(g * share, 8), share)
            t_scale = scale[pl.ds(pl.multiple_of(s_tiles * LANES + g * 8, 8), 8), :1]
            prob = t_exp[at_t, :] * t_scale
            value = s_exp[at_s, :] * scale[at_s, :1]
            for a in range(images):
                out.append(value[8 * a : 8 * a + 8] - partner_of(prob, a, position))
        both = pl.ds(pl.multiple_of(i * 2 * share, 16), 2 * share)
        grads[both, :] = jnp.concatenate(out, axis=0).astype(BF16)

    @pl.loop(0, tiles)
    def _(n):
        at_n = pl.ds(pl.multiple_of(n * COLS, COLS), COLS)
        part = jnp.dot(rows_t[...], grads[:, at_n], preferred_element_type=F32)
        inverse = proto_inv[:, at_n]
        normed = proto_ref[:, at_n].astype(F32) * inverse
        along = jnp.sum(normed * part, axis=0, keepdims=True)
        part = inverse * (part - normed * along)
        raw[:, :, :, at_n] = part.reshape(NX * NZL, NC, 16, COLS)
        wire_c[:, :, at_n] = raw[:, pl.ds(1 - c, 1), :, at_n].reshape(NX * NZL, 16, COLS).astype(BF16)

    over = []
    for k in sorted(range(NX), key=lambda k: -min(k, NX - k)):
        at_k = pl.ds(wrap(x + k, NX) * NZL, NZL)
        over.append(send(wire_c.at[at_k], land_c.at[at_k], at(c_=1 - c)))

    s_value, t_value = s_chunk[zh], t_chunk[zh]
    for k in range(1, NZH):
        s_met[k - 1].wait_recv()
        t_met[k - 1].wait_recv()
        s_value = s_value + s_land_z[k].astype(F32)
        t_value = t_value + t_land_z[k]
    at_s = pl.ds(pl.multiple_of(f * share, 8), share)
    s_value = s_value * scale[at_s, :1]
    t_value = t_value * scale[pl.ds(pl.multiple_of(s_tiles * LANES + f * 8, 8), 8), :1]
    position = lax.broadcasted_iota(jnp.int32, (STUDENT_CROPS, bot), 0)
    value = s_value - jnp.concatenate(
        [partner_of(t_value, a, position) for a in range(images)], axis=0
    )
    normed = unit[at_s, :]
    value = value - normed * jnp.sum(normed * value, axis=1, keepdims=True)
    final[y, zh] = (value * row_inv[at_s, :1]).astype(BF16)
    final_z = along_z(final)
    final_y = along_y(final)
    final_y[0].first()

    for copy in over:
        copy.wait_recv()

    def own_raw(k):
        def own(dx):
            slot = wrap(x + dx, NX) * NZL + k
            return raw[slot, c] + land_c[slot].astype(F32)

        return own

    raw_x = [
        Gathered(send, own_raw(k), wire_x.at[k], land_x.at[k], to_x, NX, k % 2) for k in range(NZL)
    ]
    for one in raw_x:
        one.first()
        one.second()
    final_y[0].second()
    for k in order:
        final_z[k - 1].wait_recv()
        final_y[k].first()
    for k in range(NZL):
        own_x[k] = raw_x[k].total()
    raw_met = []
    for k in range(1, NZL):
        wire_l[k] = own_x[wrap(zl + k, NZL)].astype(BF16)
        raw_met.append(send(wire_l.at[k], land_l.at[k], to_zl(k)))
    for k in order:
        final_y[k].second()
    value = own_x[zl]
    for k in range(1, NZL):
        raw_met[k - 1].wait_recv()
        value = value + land_l[k].astype(F32)
    raw_ref[...] = value
    for one in final_y:
        one.last()
    for i in range(NY):
        feat_ref[i * y_rows : (i + 1) * y_rows, :] = final[i].astype(F32).reshape(y_rows, bot)

    for copy in started:
        copy.wait_send()


def call(pack, proto, teacher, center, s_rows, t_rows):
    bot, count = proto.shape
    y_rows = s_rows // NY
    z_rows = y_rows // NZH
    width = pack.shape[1]
    vmem = pltpu.VMEM
    s_pad, t_pad = up(s_rows, LANES), up(t_rows, LANES)
    copies = (
        (NZL * NC - 1) + (NX - 1) + (NZH - 1) + NZH * (NY - 1)
        + (NZL - 1) + NZL * (NX - 1) + NZL * NX
        + (NY - 1) + (NZH - 1)
        + 3 * (NY - 1) + 2 * (NZH - 1) + (NZH - 1) + NZH * (NY - 1)
        + NX + NZL * (NX - 1) + (NZL - 1)
    )
    return pl.pallas_call(
        kernel,
        out_shape=(
            jax.ShapeDtypeStruct((16, count), F32),
            jax.ShapeDtypeStruct((s_rows, bot), F32),
            jax.ShapeDtypeStruct((16, count), F32),
        ),
        in_specs=[pl.BlockSpec(memory_space=pltpu.VMEM)] * 4,
        out_specs=[pl.BlockSpec(memory_space=pltpu.VMEM)] * 3,
        scratch_shapes=[
            vmem((NZL * NC, 8, count // 8), F32),
            vmem((NX, 8, count // 8), F32),
            vmem((NY, NZH, 16, width), BF16),
            vmem((NX * NZL * NC, 16, count), BF16),
            vmem((bot, count), BF16),
            vmem((count, bot), BF16),
            vmem((1, count), F32),
            vmem((s_rows, bot), F32),
            vmem((s_rows, bot), BF16),
            vmem((bot, s_rows), BF16),
            vmem((s_rows, LANES), F32),
            vmem((t_pad, bot), BF16),
            vmem((s_rows, count), F32),
            vmem((t_pad, count), F32),
            vmem((s_pad, LANES), F32),
            vmem((t_pad, LANES), F32),
            vmem((s_pad + t_pad, LANES), F32),
            vmem((NY, 8, LANES), F32),
            vmem((NZH, 8, LANES), F32),
            vmem((s_rows, count), BF16),
            vmem((s_rows, bot), F32),
            vmem((t_pad, bot), F32),
            vmem((2, 2, 4, y_rows // 2, bot), BF16),
            vmem((2, 2, 4, y_rows // 2, bot), BF16),
            vmem((2, 4, 8 * NZH, bot), F32),
            vmem((2, 4, 8 * NZH, bot), F32),
            vmem((NZH, z_rows, bot), F32),
            vmem((NZH, z_rows, bot), BF16),
            vmem((NZH, z_rows, bot), BF16),
            vmem((NZH, 8, bot), F32),
            vmem((NZH, 8, bot), F32),
            vmem((NY, NZH, z_rows, bot), BF16),
            vmem((NX * NZL, NC, 16, count), F32),
            vmem((NX * NZL, 16, count), BF16),
            vmem((NX * NZL, 16, count), BF16),
            vmem((NZL, 2, 4, 16, count), BF16),
            vmem((NZL, 2, 4, 16, count), BF16),
            vmem((NZL, 16, count), F32),
            vmem((NZL, 16, count), BF16),
            vmem((NZL, 16, count), BF16),
            pltpu.SemaphoreType.DMA((copies,)),
            pltpu.SemaphoreType.DMA((copies,)),
        ],
        compiler_params=pltpu.CompilerParams(
            collective_id=0, has_side_effects=True, vmem_limit_bytes=56 * 1024 * 1024
        ),
    )(pack, proto, teacher, center)


def body(student_feat, teacher_feat, student_proto, teacher_proto, center):
    s_rows, t_rows = student_feat.shape[0], teacher_feat.shape[0]
    t_pad = up(t_rows, LANES)
    width = max(s_rows, 3 * t_pad)
    student_t, teacher_t = student_feat.T, teacher_feat.T
    pieces = [jnp.pad(teacher_t[4 * q : 4 * q + 4], ((0, 0), (0, t_pad - t_rows))) for q in range(3)]
    pieces = jnp.concatenate(pieces, axis=1)
    pack = jnp.concatenate(
        [
            jnp.pad(student_t, ((0, 0), (0, width - s_rows))),
            jnp.pad(pieces, ((0, 0), (0, width - 3 * t_pad))),
        ],
        axis=0,
    )
    return tuple(call(pack, student_proto, teacher_proto, center.reshape(1, -1), s_rows, t_rows))


def solution(mesh):
    placed = (P("dp", "fsdp"), P("dp", "fsdp"), P(None, "fsdp"), P("dp", "fsdp"), P("fsdp"))
    return jax.shard_map(
        body,
        mesh=mesh,
        in_specs=placed,
        out_specs=(P("dp", "fsdp"), P("dp", None), P("dp", "fsdp")),
        check_vma=False,
    )
```

time: 123 us -> 100 us (0.81)
  the two profiles are of different devices: /device:TPU:16 before, /device:TPU:8 now
where the time goes in v2:
time: 100 us; the launch traced here: 99.7 us
  Pallas kernels  92.3 us (92%)
  local copies, waits for them, and re-layouts  5.39 us (5%)
  other arithmetic  1.36 us (1%)
    pallas_call x1, Pallas kernels, call(): pl.pallas_call(kernel, out_shape=(jax.ShapeDtypeStruct((16, count), F32),...  92.3 us
    unnamed x5, local copies, waits for them, and re-layouts  4.62 us

profile of v2, /device:TPU:8, one launch (start us, length us, event | category | flops | bytes accessed | tf_op | source)
XLA Modules:
  0.0 99.7 jit_solution(3767184639497349249)
XLA Ops:
  0.6 0.8 fusion.13
  1.4 1.4 %fusion.11.pack_ref = bf16[16,768]{1,0:T(8,128)(2,1)} fusion(bf16[4,192]{1,0:T(4,128)(2,1)S(1)} %get-tuple-element.4, bf16[4,192]{1,0:T(4,128)(2,1)S(1)} %get-tuple-element.5, bf16[4,192]{1,0:T(4,128)(2,1)S(1)} %get-tuple-element.3, bf16[12,768]{1,0:T(8,128)(2,1)} %bitcast.3), kind=kLoop, calls=%fused_computation.16 | loop fusion | flops 282624 | bytes 47616 | tf_op jit(solution)/shard_map/concatenate | solution.py:562
  2.8 92.3 %shard_map.76 = (f32[16,2048]{1,0:T(8,128)}, f32[768,384]{1,0:T(8,128)}, f32[16,2048]{1,0:T(8,128)}) custom-call(bf16[16,768]{1,0:T(8,128)(2,1)} %fusion.11.pack_ref, bf16[384,2048]{1,0:T(8,128)(2,1)} %proto_ref.1, f32[16,2048]{1,0:T(8,128)} %teacher_ref.1, f32[1,2048]{1,0:T(1,128)} %bitcast.4), custom_call_target="tpu_custom_call" | custom-call | tf_op jit(solution)/shard_map/pallas_call | solution.py:496
  95.0 1.6 %copy.11 = f32[16,2048]{1,0:T(8,128)} copy(f32[16,2048]{1,0:T(8,128)} %get-tuple-element.9) | data formatting | bytes 262144
  96.6 0.0 copy-start
  96.6 2.4 %copy.12 = f32[768,384]{1,0:T(8,128)} copy(f32[768,384]{1,0:T(8,128)} %get-tuple-element.10) | data formatting | bytes 2359296
  99.0 0.0 copy-done
  99.0 0.7 copy.13
Async XLA Ops:
  96.6 2.4 %copy-start = (f32[16,2048]{1,0:T(8,128)S(1)}, f32[16,2048]{1,0:T(8,128)}, u32[]{:S(2)}) copy-start(f32[16,2048]{1,0:T(8,128)} %get-tuple-element.11) | copy-start | bytes 393220

commit v3 on v2

--- a/solution.py
+++ b/solution.py
@@ -33,19 +33,19 @@
 
 
 class Spread:
-    def __init__(self, send, spot, to, size, odd):
-        self.send, self.spot, self.to = send, spot, to
+    def __init__(self, send, spot, to, size, odd, straight=2):
+        self.send, self.spot, self.to, self.straight = send, spot, to, straight
         self.reach = dict(zip((1, -1), hops(size, odd)))
         self.out = {}
 
     def first(self):
         for way in (1, -1):
-            for s in range(min(2, self.reach[way]), 0, -1):
+            for s in range(min(self.straight, self.reach[way]), 0, -1):
                 self.out[way, s] = self.send(self.spot(0), self.spot(0), self.to(way * s))
 
     def second(self):
         for way in (1, -1):
-            if self.reach[way] > 2:
+            if self.reach[way] > self.straight:
                 self.out[way, 2].wait_recv()
                 block = self.spot(-2 * way)
                 for s in range(self.reach[way] - 2, 0, -1):
@@ -54,7 +54,7 @@
     def arrivals(self):
         for way in (1, -1):
             for s in range(1, self.reach[way] + 1):
-                if not (s == 2 and self.reach[way] > 2):
+                if not (s == 2 and self.reach[way] > self.straight):
                     yield self.out[way, s], self.spot(-way * s)
 
     def last(self):
@@ -109,8 +109,8 @@
 
 
 def kernel(
-    pack_ref, proto_ref, teacher_ref, center_ref, new_ref, feat_ref, raw_ref,
-    norm_near, norm_x, feats, masters, half, half_t, proto_inv, unit, rows, rows_t, row_inv,
+    student_ref, teacher_feat_ref, proto_ref, teacher_ref, center_ref, new_ref, feat_ref, raw_ref,
+    feats, masters, half, half_t, proto_inv, unit, rows, rows_t, row_inv,
     t_rows, s_exp, t_exp, s_sum, t_sum, scale, den_y, den_z, grads, s_part, t_part,
     s_wire, s_land, t_wire, t_land, s_chunk, s_wire_z, s_land_z, t_chunk, t_land_z, final,
     raw, wire_c, land_c, wire_x, land_x, own_x, wire_l, land_l,
@@ -122,7 +122,7 @@
     bot, count = proto_ref.shape
     s_rows = unit.shape[0]
     t_pad = t_sum.shape[0]
-    width = pack_ref.shape[1]
+    width = feats.shape[3]
     tiles = count // COLS
     s_tiles, t_tiles = s_sum.shape[0] // LANES, t_pad // LANES
     share = s_rows // (NY * NZH)
@@ -161,34 +161,42 @@
         started.append(copy)
         return copy
 
-    near = [
-        at(zl_=wrap(zl + k, NZL), c_=lax.rem(c + e, NC))
-        for k in range(NZL)
-        for e in range(NC)
-        if k or e
-    ]
     partners = (
         [to_y(k) for k in range(1, NY)]
         + [to_zh(k) for k in range(1, NZH)]
-        + near
+        + [to_zl(k) for k in range(1, NZL)]
+        + [at(c_=1 - c)]
         + [to_x(k) for k in range(1, NX)]
     )
     barrier = pltpu.get_barrier_semaphore()
     for partner in partners:
         pl.semaphore_signal(barrier, inc=1, device_id=partner, device_id_type=MESH)
 
-    feats[y, zh] = pack_ref[...]
+    teacher_feat = teacher_feat_ref[...].astype(F32)
+    wide = [student_ref[...].astype(F32)]
+    if width > s_rows:
+        wide.append(jnp.zeros((12, width - s_rows), F32))
+    slot = jnp.concatenate(
+        [jnp.concatenate(wide, axis=1), jnp.zeros((4, width), F32)], axis=0
+    )
+    t_count = teacher_feat.shape[1]
+    fill = [jnp.zeros((4, t_pad - t_count), F32)] if t_pad > t_count else []
+    last = []
+    for q in range(3):
+        last += [teacher_feat[4 * q : 4 * q + 4]] + fill
+    if width > 3 * t_pad:
+        last.append(jnp.zeros((4, width - 3 * t_pad), F32))
+    last = jnp.concatenate(last, axis=1)
+    low = jnp.concatenate([jnp.zeros((4, width), F32), last], axis=0)
+    line = lax.broadcasted_iota(jnp.int32, (16, width), 0)
+    feats[y, zh] = jnp.where(
+        line < 12, slot, jnp.concatenate([jnp.zeros((8, width), F32), low], axis=0)
+    ).astype(BF16)
     student_own = proto_ref[pl.ds(pl.multiple_of(d * 16, 16), 16), :].astype(F32)
     own_master = MOMENTUM * teacher_ref[...] + (1.0 - MOMENTUM) * student_own
     new_ref[...] = own_master
-    squares = jnp.sum(own_master * own_master, axis=0, keepdims=True)
-    line = lax.broadcasted_iota(jnp.int32, (8, count // 8), 0)
-    folded = jnp.zeros((8, count // 8), F32)
-    for i in range(8):
-        folded = jnp.where(line == i, squares[:, i * (count // 8) : (i + 1) * (count // 8)], folded)
-    norm_near[0] = folded
+    masters[d] = own_master
     pl.semaphore_wait(barrier, len(partners))
-    norms = [send(norm_near.at[0], norm_near.at[i + 1], to) for i, to in enumerate(near)]
 
     def along_z(buffer):
         return [send(buffer.at[y, zh], buffer.at[y, zh], to_zh(k)) for k in range(1, NZH)]
@@ -197,12 +205,28 @@
         def spot_of(k):
             return lambda dy: buffer.at[wrap(y + dy, NY), wrap(zh - k, NZH)]
 
-        return [Spread(send, spot_of(k), to_y, NY, k % 2) for k in range(NZH)]
+        return [
+            Spread(send, spot_of(k), to_y, NY, k % 2, NY if 2 * k == NZH else 2)
+            for k in range(NZH)
+        ]
 
     order = sorted(range(1, NZH), key=lambda k: (min(k, NZH - k), k))
     feat_z = along_z(feats)
     feat_y = along_y(feats)
     feat_y[0].first()
+
+    across = []
+
+    def to_sibling(block):
+        across.append(send(block, block, at(c_=1 - c)))
+
+    def master_of(k):
+        return lambda dx: masters.at[(wrap(x + dx, NX) * NZL + wrap(zl - k, NZL)) * NC + c]
+
+    master_z = [send(masters.at[d], masters.at[d], to_zl(k)) for k in range(1, NZL)]
+    master_x = [Spread(send, master_of(k), to_x, NX, k % 2) for k in range(NZL)]
+    master_x[0].first()
+    to_sibling(masters.at[d])
 
     @pl.loop(0, tiles)
     def _(n):
@@ -214,43 +238,21 @@
         half_t[at_n, :] = normed.T.astype(BF16)
         proto_inv[:, at_n] = inverse
 
-    for copy in norms:
-        copy.wait_recv()
-    norm_x[0] = jnp.sum(norm_near[...], axis=0)
-    norms = [send(norm_x.at[0], norm_x.at[k], to_x(k)) for k in range(1, NX)]
     feat_y[0].second()
     for k in order:
         feat_z[k - 1].wait_recv()
         feat_y[k].first()
-    for copy in norms:
-        copy.wait_recv()
-    inverse = lax.rsqrt(jnp.sum(norm_x[...], axis=0) + EPSILON)
-    inverse = jnp.concatenate([inverse[i : i + 1] for i in range(8)], axis=1)
-    masters[d] = (own_master * inverse).astype(BF16)
-
-    across = []
-
-    def to_sibling(block):
-        across.append(send(block, block, at(c_=1 - c)))
-
-    def master_of(k):
-        return lambda dx: masters.at[(wrap(x + dx, NX) * NZL + wrap(zl - k, NZL)) * NC + c]
-
-    master_z = [send(masters.at[d], masters.at[d], to_zl(k)) for k in range(1, NZL)]
-    master_x = [Spread(send, master_of(k), to_x, NX, k % 2) for k in range(NZL)]
-    master_x[0].first()
-    to_sibling(masters.at[d])
-    for k in order:
-        feat_y[k].second()
     for k in range(1, NZL):
         master_z[k - 1].wait_recv()
         master_x[k].first()
         to_sibling(master_of(k)(0))
-    for one in feat_y:
-        one.last()
+    for k in order:
+        feat_y[k].second()
     for copy, block in master_x[0].arrivals():
         copy.wait_recv()
         to_sibling(block)
+    for one in feat_y:
+        one.last()
 
     slots = feats[...].reshape(NY * NZH * 16, width)
     spots = lax.broadcasted_iota(jnp.int32, (bot, NY * NZH * 16), 1)
@@ -294,8 +296,7 @@
     s_part[...] = jnp.zeros_like(s_part)
     t_part[...] = jnp.zeros_like(t_part)
 
-    @pl.loop(0, tiles)
-    def _(n):
+    def student_tile(n):
         at_n = pl.ds(pl.multiple_of(n * COLS, COLS), COLS)
         logits = jnp.dot(rows[...], half[:, at_n], preferred_element_type=F32)
         value = jnp.exp(logits * (1.0 / STUDENT_TEMP))
@@ -303,6 +304,17 @@
         s_sum[:s_rows, :] += fold(value)
         s_part[...] += jnp.dot(value.astype(BF16), half_t[at_n, :], preferred_element_type=F32)
 
+    def masters_on(k):
+        for copy, block in master_x[k].arrivals():
+            copy.wait_recv()
+            to_sibling(block)
+
+    early = tiles * 5 // 8
+    pl.loop(0, early)(student_tile)
+    if NZL > 1:
+        masters_on(1)
+    pl.loop(early, tiles)(student_tile)
+
     part = s_part[...]
     s_part[...] = part - unit[...] * jnp.sum(unit[...] * part, axis=1, keepdims=True)
 
@@ -321,10 +333,8 @@
     ]
     for one in s_ring:
         one.first()
-    for k in range(1, NZL):
-        for copy, block in master_x[k].arrivals():
-            copy.wait_recv()
-            to_sibling(block)
+    for k in range(2, NZL):
+        masters_on(k)
     for copy in across:
         copy.wait_recv()
 
@@ -332,7 +342,8 @@
     def _(n):
         at_n = pl.ds(pl.multiple_of(n * COLS, COLS), COLS)
         block = masters[:, :, at_n].reshape(bot, COLS)
-        logits = jnp.dot(t_rows[...], block, preferred_element_type=F32)
+        inverse = lax.rsqrt(jnp.sum(block * block, axis=0, keepdims=True) + EPSILON)
+        logits = jnp.dot(t_rows[...], (block * inverse).astype(BF16), preferred_element_type=F32)
         value = jnp.exp((logits - center_ref[:, at_n]) * (1.0 / TEACHER_TEMP))
         t_exp[:, at_n] = value
         t_sum[...] += fold(value)
@@ -341,8 +352,6 @@
     def own_t(dy):
         return t_part[pl.ds(pl.multiple_of(wrap(y + dy, NY) * (8 * NZH), 8), 8 * NZH), :]
 
-    t_ring = Gathered(send, own_t, t_wire, t_land, to_y, NY, 1)
-    t_ring.first()
     line = lax.broadcasted_iota(jnp.int32, (8, LANES), 0)
     packed = jnp.zeros((8, LANES), F32)
     for i in range(s_tiles + t_tiles):
@@ -354,6 +363,8 @@
         packed = jnp.where(line == i, jnp.sum(block.T, axis=0, keepdims=True), packed)
     den_y[0] = packed
     dens = [send(den_y.at[0], den_y.at[k], to_y(k)) for k in range(1, NY)]
+    t_ring = Gathered(send, own_t, t_wire, t_land, to_y, NY, 1)
+    t_ring.first()
     for one in s_ring:
         one.second()
     t_ring.second()
@@ -401,21 +412,52 @@
         both = pl.ds(pl.multiple_of(i * 2 * share, 16), 2 * share)
         grads[both, :] = jnp.concatenate(out, axis=0).astype(BF16)
 
-    @pl.loop(0, tiles)
-    def _(n):
-        at_n = pl.ds(pl.multiple_of(n * COLS, COLS), COLS)
-        part = jnp.dot(rows_t[...], grads[:, at_n], preferred_element_type=F32)
-        inverse = proto_inv[:, at_n]
-        normed = proto_ref[:, at_n].astype(F32) * inverse
-        along = jnp.sum(normed * part, axis=0, keepdims=True)
-        part = inverse * (part - normed * along)
-        raw[:, :, :, at_n] = part.reshape(NX * NZL, NC, 16, COLS)
-        wire_c[:, :, at_n] = raw[:, pl.ds(1 - c, 1), :, at_n].reshape(NX * NZL, 16, COLS).astype(BF16)
+    wide = count // 2
+
+    def proto_tile(q):
+        def tile(n):
+            at_n = pl.ds(pl.multiple_of(n * COLS, COLS), COLS)
+            at_q = pl.ds(pl.multiple_of(n * COLS - q * wide, COLS), COLS)
+            part = jnp.dot(rows_t[...], grads[:, at_n], preferred_element_type=F32)
+            inverse = proto_inv[:, at_n]
+            normed = proto_ref[:, at_n].astype(F32) * inverse
+            along = jnp.sum(normed * part, axis=0, keepdims=True)
+            part = inverse * (part - normed * along)
+            raw[q, :, :, :, at_q] = part.reshape(NX * NZL, NC, 16, COLS)
+            wire_c[q, :, :, at_q] = (
+                raw[q, :, pl.ds(1 - c, 1), :, at_q].reshape(NX * NZL, 16, COLS).astype(BF16)
+            )
+
+        return tile
+
+    def own_raw(q, k):
+        def own(dx):
+            slot = wrap(x + dx, NX) * NZL + k
+            return raw[q, slot, c] + land_c[q, slot].astype(F32)
+
+        return own
 
     over = []
-    for k in sorted(range(NX), key=lambda k: -min(k, NX - k)):
-        at_k = pl.ds(wrap(x + k, NX) * NZL, NZL)
-        over.append(send(wire_c.at[at_k], land_c.at[at_k], at(c_=1 - c)))
+    raw_x = []
+    for q in range(2):
+        pl.loop(q * tiles // 2, (q + 1) * tiles // 2)(proto_tile(q))
+        over.append(send(wire_c.at[q], land_c.at[q], at(c_=1 - c)))
+        raw_x.append(
+            [
+                Gathered(
+                    send, own_raw(q, k), wire_x.at[q, k], land_x.at[q, k], to_x, NX, (k + q) % 2
+                )
+                for k in range(NZL)
+            ]
+        )
+
+    def on_x(q):
+        over[q].wait_recv()
+        for one in raw_x[q]:
+            one.first()
+            one.second()
+
+    on_x(0)
 
     s_value, t_value = s_chunk[zh], t_chunk[zh]
     for k in range(1, NZH):
@@ -437,39 +479,27 @@
     final_y = along_y(final)
     final_y[0].first()
 
-    for copy in over:
-        copy.wait_recv()
-
-    def own_raw(k):
-        def own(dx):
-            slot = wrap(x + dx, NX) * NZL + k
-            return raw[slot, c] + land_c[slot].astype(F32)
-
-        return own
-
-    raw_x = [
-        Gathered(send, own_raw(k), wire_x.at[k], land_x.at[k], to_x, NX, k % 2) for k in range(NZL)
-    ]
-    for one in raw_x:
-        one.first()
-        one.second()
+    on_x(1)
     final_y[0].second()
     for k in order:
         final_z[k - 1].wait_recv()
         final_y[k].first()
-    for k in range(NZL):
-        own_x[k] = raw_x[k].total()
     raw_met = []
-    for k in range(1, NZL):
-        wire_l[k] = own_x[wrap(zl + k, NZL)].astype(BF16)
-        raw_met.append(send(wire_l.at[k], land_l.at[k], to_zl(k)))
-    for k in order:
-        final_y[k].second()
-    value = own_x[zl]
-    for k in range(1, NZL):
-        raw_met[k - 1].wait_recv()
-        value = value + land_l[k].astype(F32)
-    raw_ref[...] = value
+    for q in range(2):
+        for k in range(NZL):
+            own_x[q, k] = raw_x[q][k].total()
+        for k in range(1, NZL):
+            wire_l[q, k] = own_x[q, wrap(zl + k, NZL)].astype(BF16)
+            raw_met.append(send(wire_l.at[q, k], land_l.at[q, k], to_zl(k)))
+        if q == 0:
+            for k in order:
+                final_y[k].second()
+    for q in range(2):
+        value = own_x[q, zl]
+        for k in range(1, NZL):
+            raw_met[q * (NZL - 1) + k - 1].wait_recv()
+            value = value + land_l[q, k].astype(F32)
+        raw_ref[:, q * wide : (q + 1) * wide] = value
     for one in final_y:
         one.last()
     for i in range(NY):
@@ -479,19 +509,20 @@
         copy.wait_send()
 
 
-def call(pack, proto, teacher, center, s_rows, t_rows):
+def call(student, teacher_feat, proto, teacher, center):
     bot, count = proto.shape
+    s_rows, t_rows = student.shape[1], teacher_feat.shape[1]
     y_rows = s_rows // NY
     z_rows = y_rows // NZH
-    width = pack.shape[1]
     vmem = pltpu.VMEM
     s_pad, t_pad = up(s_rows, LANES), up(t_rows, LANES)
+    width = max(s_rows, 3 * t_pad)
     copies = (
-        (NZL * NC - 1) + (NX - 1) + (NZH - 1) + NZH * (NY - 1)
+        (NZH - 1) + NZH * (NY - 1)
         + (NZL - 1) + NZL * (NX - 1) + NZL * NX
         + (NY - 1) + (NZH - 1)
         + 3 * (NY - 1) + 2 * (NZH - 1) + (NZH - 1) + NZH * (NY - 1)
-        + NX + NZL * (NX - 1) + (NZL - 1)
+        + 2 + 2 * NZL * (NX - 1) + 2 * (NZL - 1)
     )
     return pl.pallas_call(
         kernel,
@@ -500,13 +531,11 @@
             jax.ShapeDtypeStruct((s_rows, bot), F32),
             jax.ShapeDtypeStruct((16, count), F32),
         ),
-        in_specs=[pl.BlockSpec(memory_space=pltpu.VMEM)] * 4,
+        in_specs=[pl.BlockSpec(memory_space=pltpu.VMEM)] * 5,
         out_specs=[pl.BlockSpec(memory_space=pltpu.VMEM)] * 3,
         scratch_shapes=[
-            vmem((NZL * NC, 8, count // 8), F32),
-            vmem((NX, 8, count // 8), F32),
             vmem((NY, NZH, 16, width), BF16),
-            vmem((NX * NZL * NC, 16, count), BF16),
+            vmem((NX * NZL * NC, 16, count), F32),
             vmem((bot, count), BF16),
             vmem((count, bot), BF16),
             vmem((1, count), F32),
@@ -535,38 +564,27 @@
             vmem((NZH, 8, bot), F32),
             vmem((NZH, 8, bot), F32),
             vmem((NY, NZH, z_rows, bot), BF16),
-            vmem((NX * NZL, NC, 16, count), F32),
-            vmem((NX * NZL, 16, count), BF16),
-            vmem((NX * NZL, 16, count), BF16),
-            vmem((NZL, 2, 4, 16, count), BF16),
-            vmem((NZL, 2, 4, 16, count), BF16),
-            vmem((NZL, 16, count), F32),
-            vmem((NZL, 16, count), BF16),
-            vmem((NZL, 16, count), BF16),
+            vmem((2, NX * NZL, NC, 16, count // 2), F32),
+            vmem((2, NX * NZL, 16, count // 2), BF16),
+            vmem((2, NX * NZL, 16, count // 2), BF16),
+            vmem((2, NZL, 2, 2, 16, count // 2), BF16),
+            vmem((2, NZL, 2, 2, 16, count // 2), BF16),
+            vmem((2, NZL, 16, count // 2), F32),
+            vmem((2, NZL, 16, count // 2), BF16),
+            vmem((2, NZL, 16, count // 2), BF16),
             pltpu.SemaphoreType.DMA((copies,)),
             pltpu.SemaphoreType.DMA((copies,)),
         ],
         compiler_params=pltpu.CompilerParams(
             collective_id=0, has_side_effects=True, vmem_limit_bytes=56 * 1024 * 1024
         ),
-    )(pack, proto, teacher, center)
+    )(student, teacher_feat, proto, teacher, center)
 
 
 def body(student_feat, teacher_feat, student_proto, teacher_proto, center):
-    s_rows, t_rows = student_feat.shape[0], teacher_feat.shape[0]
-    t_pad = up(t_rows, LANES)
-    width = max(s_rows, 3 * t_pad)
-    student_t, teacher_t = student_feat.T, teacher_feat.T
-    pieces = [jnp.pad(teacher_t[4 * q : 4 * q + 4], ((0, 0), (0, t_pad - t_rows))) for q in range(3)]
-    pieces = jnp.concatenate(pieces, axis=1)
-    pack = jnp.concatenate(
-        [
-            jnp.pad(student_t, ((0, 0), (0, width - s_rows))),
-            jnp.pad(pieces, ((0, 0), (0, width - 3 * t_pad))),
-        ],
-        axis=0,
-    )
-    return tuple(call(pack, student_proto, teacher_proto, center.reshape(1, -1), s_rows, t_rows))
+    return tuple(
+        call(student_feat.T, teacher_feat.T, student_proto, teacher_proto, center.reshape(1, -1))
+    )
 
 
 def solution(mesh):

time: 100 us -> 97.7 us (0.977)
  other arithmetic: 1.36 us -> 0 us
    concatenate x1 -> x0, other arithmetic: 1.36 us -> none  [body(): jnp.concatenate([jnp.pad(student_t, ((0, 0), (0, width - s_rows))), jnp.p...]
where the time goes in v3:
time: 97.7 us; the launch traced here: 97.5 us
  Pallas kernels  92.2 us (94%)
  local copies, waits for them, and re-layouts  4.62 us (5%)
    pallas_call x1, Pallas kernels, call(): pl.pallas_call(kernel, out_shape=(jax.ShapeDtypeStruct((16, count), F32),...  92.2 us
    unnamed x5, local copies, waits for them, and re-layouts  4.62 us

profile of v3, /device:TPU:8, one launch (start us, length us, event | category | flops | bytes accessed | tf_op | source)
XLA Modules:
  0.0 97.5 jit_solution(9964343628899655791)
XLA Ops:
  0.6 92.2 %shard_map.76 = (f32[16,2048]{1,0:T(8,128)}, f32[768,384]{1,0:T(8,128)}, f32[16,2048]{1,0:T(8,128)}) custom-call(bf16[12,768]{1,0:T(8,128)(2,1)} %bitcast.3, bf16[12,192]{1,0:T(8,128)(2,1)} %bitcast.4, bf16[384,2048]{1,0:T(8,128)(2,1)} %proto_ref.1, f32[16,2048]{1,0:T(8,128)} %teacher_ref.1, f32[1,2048]{1,0:T(1,128)} %bitcast.5), custom_call_target="tpu_custom_call" | custom-call | tf_op jit(solution)/shard_map/pallas_call | solution.py:527
  92.9 1.6 %copy.11 = f32[16,2048]{1,0:T(8,128)} copy(f32[16,2048]{1,0:T(8,128)} %get-tuple-element.6) | data formatting | bytes 262144
  94.4 0.0 copy-start
  94.4 2.4 %copy.12 = f32[768,384]{1,0:T(8,128)} copy(f32[768,384]{1,0:T(8,128)} %get-tuple-element.7) | data formatting | bytes 2359296
  96.8 0.0 copy-done
  96.8 0.7 copy.13
Async XLA Ops:
  94.4 2.4 %copy-start = (f32[16,2048]{1,0:T(8,128)S(1)}, f32[16,2048]{1,0:T(8,128)}, u32[]{:S(2)}) copy-start(f32[16,2048]{1,0:T(8,128)} %get-tuple-element.8) | copy-start | bytes 393220

commit v4 on v3

--- a/solution.py
+++ b/solution.py
@@ -17,7 +17,8 @@
 TEACHER_TEMP = 0.04
 STUDENT_TEMP = 0.1
 LANES = 128
-COLS = 256
+COLS = 512
+WIDE = 1024
 MESH = pl.DeviceIdType.MESH
 F32 = jnp.float32
 BF16 = jnp.bfloat16
@@ -242,12 +243,12 @@
     for k in order:
         feat_z[k - 1].wait_recv()
         feat_y[k].first()
+    for k in order:
+        feat_y[k].second()
     for k in range(1, NZL):
         master_z[k - 1].wait_recv()
         master_x[k].first()
         to_sibling(master_of(k)(0))
-    for k in order:
-        feat_y[k].second()
     for copy, block in master_x[0].arrivals():
         copy.wait_recv()
         to_sibling(block)
@@ -289,7 +290,7 @@
     ).astype(BF16)
 
     def fold(values):
-        return values[:, :LANES] + values[:, LANES:]
+        return sum(values[:, i : i + LANES] for i in range(0, values.shape[1], LANES))
 
     s_sum[...] = jnp.zeros_like(s_sum)
     t_sum[...] = jnp.zeros_like(t_sum)
@@ -297,7 +298,7 @@
     t_part[...] = jnp.zeros_like(t_part)
 
     def student_tile(n):
-        at_n = pl.ds(pl.multiple_of(n * COLS, COLS), COLS)
+        at_n = pl.ds(pl.multiple_of(n * WIDE, WIDE), WIDE)
         logits = jnp.dot(rows[...], half[:, at_n], preferred_element_type=F32)
         value = jnp.exp(logits * (1.0 / STUDENT_TEMP))
         s_exp[:, at_n] = value
@@ -309,11 +310,11 @@
             copy.wait_recv()
             to_sibling(block)
 
-    early = tiles * 5 // 8
+    early = count // WIDE * 3 // 4
     pl.loop(0, early)(student_tile)
     if NZL > 1:
         masters_on(1)
-    pl.loop(early, tiles)(student_tile)
+    pl.loop(early, count // WIDE)(student_tile)
 
     part = s_part[...]
     s_part[...] = part - unit[...] * jnp.sum(unit[...] * part, axis=1, keepdims=True)
@@ -338,10 +339,10 @@
     for copy in across:
         copy.wait_recv()
 
-    @pl.loop(0, tiles)
+    @pl.loop(0, count // WIDE)
     def _(n):
-        at_n = pl.ds(pl.multiple_of(n * COLS, COLS), COLS)
-        block = masters[:, :, at_n].reshape(bot, COLS)
+        at_n = pl.ds(pl.multiple_of(n * WIDE, WIDE), WIDE)
+        block = masters[:, :, at_n].reshape(bot, WIDE)
         inverse = lax.rsqrt(jnp.sum(block * block, axis=0, keepdims=True) + EPSILON)
         logits = jnp.dot(t_rows[...], (block * inverse).astype(BF16), preferred_element_type=F32)
         value = jnp.exp((logits - center_ref[:, at_n]) * (1.0 / TEACHER_TEMP))
@@ -416,16 +417,16 @@
 
     def proto_tile(q):
         def tile(n):
-            at_n = pl.ds(pl.multiple_of(n * COLS, COLS), COLS)
-            at_q = pl.ds(pl.multiple_of(n * COLS - q * wide, COLS), COLS)
+            at_n = pl.ds(pl.multiple_of(n * WIDE, WIDE), WIDE)
+            at_q = pl.ds(pl.multiple_of(n * WIDE - q * wide, WIDE), WIDE)
             part = jnp.dot(rows_t[...], grads[:, at_n], preferred_element_type=F32)
             inverse = proto_inv[:, at_n]
             normed = proto_ref[:, at_n].astype(F32) * inverse
             along = jnp.sum(normed * part, axis=0, keepdims=True)
             part = inverse * (part - normed * along)
-            raw[q, :, :, :, at_q] = part.reshape(NX * NZL, NC, 16, COLS)
+            raw[q, :, :, :, at_q] = part.reshape(NX * NZL, NC, 16, WIDE)
             wire_c[q, :, :, at_q] = (
-                raw[q, :, pl.ds(1 - c, 1), :, at_q].reshape(NX * NZL, 16, COLS).astype(BF16)
+                raw[q, :, pl.ds(1 - c, 1), :, at_q].reshape(NX * NZL, 16, WIDE).astype(BF16)
             )
 
         return tile
@@ -440,7 +441,7 @@
     over = []
     raw_x = []
     for q in range(2):
-        pl.loop(q * tiles // 2, (q + 1) * tiles // 2)(proto_tile(q))
+        pl.loop(q * wide // WIDE, (q + 1) * wide // WIDE)(proto_tile(q))
         over.append(send(wire_c.at[q], land_c.at[q], at(c_=1 - c)))
         raw_x.append(
             [
@@ -527,9 +528,9 @@
     return pl.pallas_call(
         kernel,
         out_shape=(
-            jax.ShapeDtypeStruct((16, count), F32),
-            jax.ShapeDtypeStruct((s_rows, bot), F32),
-            jax.ShapeDtypeStruct((16, count), F32),
+            pltpu.VMEM((16, count), F32),
+            pltpu.VMEM((s_rows, bot), F32),
+            pltpu.VMEM((16, count), F32),
         ),
         in_specs=[pl.BlockSpec(memory_space=pltpu.VMEM)] * 5,
         out_specs=[pl.BlockSpec(memory_space=pltpu.VMEM)] * 3,

time: 97.7 us -> 87.9 us (0.90)
  Pallas kernels: 92.2 us -> 84.7 us
  local copies, waits for them, and re-layouts: 4.62 us -> 2.33 us
    pallas_call x1, Pallas kernels: 92.2 us -> 84.7 us  [call(): pl.pallas_call(kernel, out_shape=(pltpu.VMEM((16, count), F32), pltpu.VME...]
    unnamed x5 -> x3, local copies, waits for them, and re-layouts: 4.62 us -> 2.33 us
where the time goes in v4:
time: 87.9 us; the launch traced here: 87.7 us
  Pallas kernels  84.7 us (96%)
  local copies, waits for them, and re-layouts  2.33 us (3%)
    pallas_call x1, Pallas kernels, call(): pl.pallas_call(kernel, out_shape=(pltpu.VMEM((16, count), F32), pltpu.VME...  84.7 us
    unnamed x3, local copies, waits for them, and re-layouts  2.33 us

profile of v4, /device:TPU:8, one launch (start us, length us, event | category | flops | bytes accessed | tf_op | source)
XLA Modules:
  0.0 87.7 jit_solution(11859991738278264535)
XLA Ops:
  0.6 84.7 %shard_map.76 = (f32[16,2048]{1,0:T(8,128)S(1)}, f32[768,384]{1,0:T(8,128)S(1)}, f32[16,2048]{1,0:T(8,128)S(1)}) custom-call(bf16[12,768]{1,0:T(8,128)(2,1)} %bitcast.3, bf16[12,192]{1,0:T(8,128)(2,1)} %bitcast.4, bf16[384,2048]{1,0:T(8,128)(2,1)} %proto_ref.1, f32[16,2048]{1,0:T(8,128)} %teacher_ref.1, f32[1,2048]{1,0:T(1,128)} %bitcast.5), custom_call_target="tpu_custom_call" | custom-call | tf_op jit(solution)/shard_map/pallas_call | solution.py:528
  85.4 0.7 copy.11
  86.0 0.7 copy.13
  86.7 1.0 %copy.12 = f32[768,384]{1,0:T(8,128)} copy(f32[768,384]{1,0:T(8,128)S(1)} %get-tuple-element.4) | data formatting | bytes 2359296
